TPU v7x, 32 devices: a whole 2x2x4 slice. The times are simulated.
32 devices in a mesh: expert: 4 (over y, x), fsdp: 8 (over z, core).
Axes of the slice: x: 2, y: 2, z: 4, core: 2. Of those that a mesh axis runs over, the one named last changes fastest.
Arguments:
- tokens: bfloat16 [1024, 6144], P('fsdp', 'expert'), may hold values from -6 to 6
- cotangent: bfloat16 [1024, 6144], P('fsdp', 'expert'), may hold values from -6 to 6
- routed_experts: int32 [1024, 2], replicated, may hold values from 0 to 7, as said below
- route_weights: float32 [1024, 2], P('fsdp'), may hold values from 0.25 to 1
- gate_matrix: bfloat16 [6144, 32768], P(None, ('expert', 'fsdp')), may hold values from -0.078125 to 0.078125
- up_matrix: bfloat16 [6144, 32768], P(None, ('expert', 'fsdp')), may hold values from -0.078125 to 0.078125
- down_matrix: bfloat16 [32768, 6144], P(('expert', 'fsdp')), may hold values from -0.09375 to 0.09375
Outputs:
- layer_output: bfloat16 [1024, 6144], P('fsdp', 'expert')
- grad_tokens: bfloat16 [1024, 6144], P('fsdp', 'expert')
- grad_gate: bfloat16 [6144, 32768], P(None, ('expert', 'fsdp'))
- grad_up: bfloat16 [6144, 32768], P(None, ('expert', 'fsdp'))
- grad_down: bfloat16 [32768, 6144], P(('expert', 'fsdp'))
Inputs may be any that keep to these rules, and one draw needn't show every extreme that they name: `routed_experts`: each row names two different experts. In every aligned block of 128 rows each expert below 2 is named by at most 16 rows; one of these experts is named by exactly 16 rows in every block, and every expert below 2 is named by exactly 16 rows in at least one block.
All inputs are finite; a program needn't handle non-finite values.
Results may differ from a plain program's by a relative error of at most 0.017.
Values may be sent and summed in bfloat16 or wider, within the bound.
A program may use at most 256 MiB of HBM per device.

v0:
```python
import jax
import jax.numpy as jnp
from jax import lax
from jax.sharding import PartitionSpec as P

D = 6144
WIN = 2
TILE = 128
CAP = 16


def silu_parts(pre_gate):
    sigmoid_val = jax.nn.sigmoid(pre_gate)
    return (sigmoid_val, pre_gate * sigmoid_val)


def local(tokens, cotangent, routed_experts, route_weights, gate_matrix, up_matrix, down_matrix):
    expert_size = lax.axis_size("expert")
    group_size = lax.axis_size("fsdp")
    expert_pos = lax.axis_index("expert")
    group_pos = lax.axis_index("fsdp")
    per_expert = expert_size // WIN
    own_expert = expert_pos // per_expert
    group_rows = tokens.shape[0]
    slice_width = tokens.shape[1]
    total_slots = group_size * CAP
    hidden_width = gate_matrix.shape[1]
    bf_zero = jnp.zeros((), jnp.bfloat16)
    window_ids = jnp.arange(WIN, dtype=jnp.int32)
    all_ids = routed_experts.reshape(group_size, group_rows, 2)
    member_all = jnp.any(all_ids[:, :, None, :] == window_ids[None, None, :, None], axis=3).astype(
        jnp.int32
    )
    group_counts = jnp.sum(member_all, axis=1)
    own_ids = lax.dynamic_index_in_dim(all_ids, group_pos, 0, keepdims=False)
    own_hits = own_ids[:, None, :] == window_ids[None, :, None]
    own_member = jnp.any(own_hits, axis=2)
    own_count = own_member.astype(jnp.int32)
    positions = jnp.cumsum(own_count, axis=0) - own_count
    row_weight = jnp.sum(jnp.where(own_hits, route_weights[:, None, :], 0.0), axis=2)
    slot_range = jnp.arange(CAP, dtype=jnp.int32)
    matches = own_member.T[:, None, :] & (positions.T[:, None, :] == slot_range[None, :, None])
    source_row = jnp.sum(
        jnp.where(matches, jnp.arange(group_rows, dtype=jnp.int32)[None, None, :], 0), axis=2
    )
    live_slot = jnp.any(matches, axis=2)
    token_slots = jnp.where(live_slot[..., None], tokens[source_row], bf_zero)
    slot_weight = jnp.take_along_axis(row_weight.T, source_row, axis=1)
    grad_slots = jnp.where(
        live_slot[..., None],
        slot_weight[..., None] * cotangent[source_row].astype(jnp.float32),
        0.0,
    ).astype(jnp.bfloat16)
    dest_expert = jnp.arange(expert_size) // per_expert
    sent_tokens, sent_grads = (
        lax.all_to_all(token_slots[dest_expert], "expert", split_axis=0, concat_axis=2, tiled=True),
        lax.all_to_all(grad_slots[dest_expert], "expert", split_axis=0, concat_axis=2, tiled=True),
    )
    token_rows, grad_rows = (
        lax.all_gather(sent_tokens, "fsdp", axis=0, tiled=True),
        lax.all_gather(sent_grads, "fsdp", axis=0, tiled=True),
    )
    token_rows = token_rows.reshape(total_slots, D)
    grad_rows = grad_rows.reshape(total_slots, D)
    expert_counts = lax.dynamic_index_in_dim(group_counts, own_expert, 1, keepdims=False)
    offsets = jnp.cumsum(expert_counts) - expert_counts
    total_rows = jnp.sum(expert_counts)
    tile_count = (total_rows + TILE - 1) // TILE
    tile_range = jnp.arange(TILE, dtype=jnp.int32)

    def tile_step(tile_pos, loop_state):
        accum_gate, accum_up, accum_down, out_buffer, back_buffer = loop_state
        places = tile_pos * TILE + tile_range
        is_valid = places < total_rows
        at_or_below = offsets[None, :] <= places[:, None]
        source_group = jnp.sum(at_or_below.astype(jnp.int32), axis=1) - 1
        group_start = jnp.max(jnp.where(at_or_below, offsets[None, :], 0), axis=1)
        slot_index = jnp.where(is_valid, source_group * CAP + places - group_start, 0)
        token_tile = jnp.where(is_valid[:, None], token_rows[slot_index], bf_zero)
        grad_tile = jnp.where(is_valid[:, None], grad_rows[slot_index], bf_zero)
        pre_gate = jnp.dot(token_tile, gate_matrix, preferred_element_type=jnp.float32)
        pre_up = jnp.dot(token_tile, up_matrix, preferred_element_type=jnp.float32)
        sigmoid_val, activated = silu_parts(pre_gate)
        hidden = (activated * pre_up).astype(jnp.bfloat16)
        out_part = jnp.dot(hidden, down_matrix, preferred_element_type=jnp.float32).astype(
            jnp.bfloat16
        )
        grad_hidden = jnp.einsum(
            "td,hd->th", grad_tile, down_matrix, preferred_element_type=jnp.float32
        )
        grad_pre_gate = (
            grad_hidden * pre_up * (sigmoid_val * (1.0 + pre_gate * (1.0 - sigmoid_val)))
        ).astype(jnp.bfloat16)
        grad_pre_up = (grad_hidden * activated).astype(jnp.bfloat16)
        back_part = jnp.einsum(
            "th,dh->td", grad_pre_gate, gate_matrix, preferred_element_type=jnp.float32
        )
        back_part = (
            back_part
            + jnp.einsum("th,dh->td", grad_pre_up, up_matrix, preferred_element_type=jnp.float32)
        ).astype(jnp.bfloat16)
        accum_gate = accum_gate + jnp.einsum(
            "td,th->dh", token_tile, grad_pre_gate, preferred_element_type=jnp.float32
        )
        accum_up = accum_up + jnp.einsum(
            "td,th->dh", token_tile, grad_pre_up, preferred_element_type=jnp.float32
        )
        accum_down = accum_down + jnp.einsum(
            "th,td->hd", hidden, grad_tile, preferred_element_type=jnp.float32
        )
        target = jnp.where(is_valid, slot_index, total_slots)
        out_buffer = out_buffer.at[target].set(out_part, mode="drop")
        back_buffer = back_buffer.at[target].set(back_part, mode="drop")
        return (accum_gate, accum_up, accum_down, out_buffer, back_buffer)

    initial = (
        jnp.zeros((D, hidden_width), jnp.float32),
        jnp.zeros((D, hidden_width), jnp.float32),
        jnp.zeros((hidden_width, D), jnp.float32),
        jnp.zeros((total_slots, D), jnp.bfloat16),
        jnp.zeros((total_slots, D), jnp.bfloat16),
    )
    accum_gate, accum_up, accum_down, out_buffer, back_buffer = lax.fori_loop(
        0, tile_count, tile_step, initial
    )
    out_got, back_got = (
        lax.all_to_all(out_buffer[None], "expert", split_axis=2, concat_axis=0, tiled=True),
        lax.all_to_all(back_buffer[None], "expert", split_axis=2, concat_axis=0, tiled=True),
    )
    out_quarter = jnp.sum(
        out_got.astype(jnp.float32).reshape(WIN, per_expert, total_slots, slice_width), axis=1
    )
    back_quarter = jnp.sum(
        back_got.astype(jnp.float32).reshape(WIN, per_expert, total_slots, slice_width), axis=1
    )
    out_expert, back_expert = (
        lax.psum_scatter(
            out_quarter.astype(jnp.bfloat16), "fsdp", scatter_dimension=1, tiled=True
        ).astype(jnp.float32),
        lax.psum_scatter(
            back_quarter.astype(jnp.bfloat16), "fsdp", scatter_dimension=1, tiled=True
        ).astype(jnp.float32),
    )
    out_flat = out_expert.reshape(WIN * CAP, slice_width)
    back_flat = back_expert.reshape(WIN * CAP, slice_width)
    layer_sum = jnp.zeros((group_rows, slice_width), jnp.float32)
    back_total = jnp.zeros((group_rows, slice_width), jnp.float32)
    for window_pos in range(WIN):
        routed_here = own_member[:, window_pos]
        gather_at = jnp.where(routed_here, window_pos * CAP + positions[:, window_pos], 0)
        layer_sum = (
            layer_sum
            + jnp.where(routed_here, row_weight[:, window_pos], 0.0)[:, None] * out_flat[gather_at]
        )
        back_total = back_total + jnp.where(routed_here[:, None], back_flat[gather_at], 0.0)
    return (
        layer_sum.astype(jnp.bfloat16),
        back_total.astype(jnp.bfloat16),
        accum_gate.astype(jnp.bfloat16),
        accum_up.astype(jnp.bfloat16),
        accum_down.astype(jnp.bfloat16),
    )


def solution(mesh):
    return jax.shard_map(
        local,
        mesh=mesh,
        in_specs=(
            P("fsdp", "expert"),
            P("fsdp", "expert"),
            P(),
            P("fsdp", None),
            P(None, ("expert", "fsdp")),
            P(None, ("expert", "fsdp")),
            P(("expert", "fsdp"), None),
        ),
        out_specs=(
            P("fsdp", "expert"),
            P("fsdp", "expert"),
            P(None, ("expert", "fsdp")),
            P(None, ("expert", "fsdp")),
            P(("expert", "fsdp"), None),
        ),
        check_vma=False,
    )
```

profile of v0, /device:TPU:0, one launch (start us, length us, event | category | flops | bytes accessed | tf_op | source)
XLA Modules:
  0.0 458.7 jit_solution(14022433789866006268)
XLA Ops:
  10.2 10.5 %all_to_all.72 = bf16[4,16,1536]{2,1,0:T(8,128)(2,1)S(1)} all-to-all(bf16[4,16,1536]{2,1,0:T(8,128)(2,1)S(1)} %gather_fusion.3), channel_id=1, replica_groups=mesh['expert'=4,'fsdp'=8] {'expert'}, dimensions={0} | all-to-all | bytes 393216 | tf_op jit(solution)/shard_map/all_to_all | solution.py:56
  24.3 7.9 %all_to_all.73 = bf16[4,16,1536]{2,1,0:T(8,128)(2,1)S(1)} all-to-all(bf16[4,16,1536]{2,1,0:T(8,128)(2,1)S(1)} %gather_fusion.5), channel_id=1, replica_groups=mesh['expert'=4,'fsdp'=8] {'expert'}, dimensions={0} | all-to-all | bytes 393216 | tf_op jit(solution)/shard_map/all_to_all | solution.py:57
  34.8 11.5 %all-gather.3.cloned.1.call-done = bf16[8,16,6144]{2,1,0:T(8,128)(2,1)} async-done(((bf16[1,16,6144]{2,1,0:T(8,128)(2,1)}), bf16[8,16,6144]{2,1,0:T(8,128)(2,1)}) %all-gather.3.cloned.1.call-update) | async-done | bytes 1572880 | tf_op jit(solution)/shard_map/all_gather | solution.py:60
  46.2 26.8 %all-gather.5.cloned.1.call-done = bf16[8,16,6144]{2,1,0:T(8,128)(2,1)} async-done(((bf16[1,16,6144]{2,1,0:T(8,128)(2,1)}), bf16[8,16,6144]{2,1,0:T(8,128)(2,1)}) %all-gather.5.cloned.1.call-update) | async-done | bytes 1572880 | tf_op jit(solution)/shard_map/all_gather | solution.py:61
  73.4 11.5 %broadcast.325.clone = f32[6144,1024]{1,0:T(8,128)} broadcast(f32[]{:T(128)} %constant.128.clone.1), dimensions={} | broadcast | bytes 25165828 | tf_op jit(solution)/shard_map/broadcast.27
  84.9 11.5 %broadcast.325 = f32[6144,1024]{1,0:T(8,128)} broadcast(f32[]{:T(128)} %constant.128.clone.1), dimensions={} | broadcast | bytes 25165828 | tf_op jit(solution)/shard_map/broadcast.27
  96.4 11.5 %broadcast_in_dim.165 = f32[1024,6144]{1,0:T(8,128)} broadcast(f32[]{:T(128)} %constant.128.clone.1), dimensions={} | broadcast | bytes 25165828 | tf_op jit(solution)/shard_map/broadcast_in_dim | solution.py:119
  107.9 156.2 %while.21 = (s32[]{:T(128)}, f32[6144,1024]{1,0:T(8,128)}, f32[6144,1024]{1,0:T(8,128)}, f32[1024,6144]{1,0:T(8,128)}, bf16[128,6144]{1,0:T(8,128)(2,1)S(1)}, /*...) while((s32[]{:T(128)}, f32[6144,1024]{1,0:T(8,128)}, ...), condition=%wide.region_14.15_spmd.clone, body=%wide.region_9.14_spmd.clone.sunk | while | flops 14523441152 | bytes 311702272 | solution.py:123
  131.0 5.8 %gather_fusion = bf16[128,6144]{1,0:T(8,128)(2,1)} fusion(bf16[128,6144]{1,0:T(8,128)(2,1)} %get-tuple-element.432, s32[1024]{0:T(1024)S(1)} %pad_clamp_fusion.6), kind=kCustom, calls=%fused_computation.clone.clone.1 | custom fusion | bytes 3146240 | tf_op jit(solution)/shard_map/while/body/gather | solution.py:79
  136.8 7.7 %fusion.72 = f32[128,1024]{1,0:T(8,128)} fusion(bf16[6144,1024]{1,0:T(8,128)(2,1)} %get-tuple-element.436, bf16[128,6144]{1,0:T(8,128)(2,1)} %gather_fusion, pred[128]{0:T(512)(128)(4,1)S(1)} %get-tuple-element.386), kind=kOutput, calls=%fused_computation.43.clone.1 | convolution fusion | flops 1611399168 | bytes 14680192 | tf_op jit(solution)/shard_map/while/body/dot_general | solution.py:81
  144.5 5.8 %gather_fusion.1 = bf16[128,6144]{1,0:T(8,128)(2,1)} fusion(bf16[128,6144]{1,0:T(8,128)(2,1)} %get-tuple-element.433, s32[1024]{0:T(1024)S(1)} %pad_clamp_fusion.6), kind=kCustom, calls=%fused_computation.1.clone.clone.1 | custom fusion | bytes 3146240 | tf_op jit(solution)/shard_map/while/body/gather | solution.py:80
  150.2 9.5 %fusion.73 = f32[128,1024]{1,0:T(8,128)S(1)} fusion(bf16[1024,6144]{1,0:T(8,128)(2,1)} %get-tuple-element.434, bf16[128,6144]{1,0:T(8,128)(2,1)} %gather_fusion.1, pred[128]{0:T(512)(128)(4,1)S(1)} %get-tuple-element.386), kind=kOutput, calls=%fused_computation.22.clone.1 | convolution fusion | flops 1611399168 | bytes 14680192 | tf_op jit(solution)/shard_map/while/body/td,hd->th/dot_general | solution.py:88
  159.8 7.5 %multiply_convert_fusion.4 = (bf16[128,1024]{1,0:T(8,128)(2,1)S(1)}, bf16[128,1024]{1,0:T(8,128)(2,1)S(1)}, bf16[128,1024]{1,0:T(8,128)(2,1)}) fusion(f32[128,1024]{1,0:T(8,128)} %fusion.72, f32[128,1024]{1,0:T(8,128)S(1)} %fusion.73, bf16[6144,1024]{1,0:T(8,128)(2,1)} %get-tuple-element.435, bf16[128,6144]{1,0:T(8,128)(2,1)S(1)} %copy-done.2, ...), kind=kOutput, calls=%fused_computation.23.clone.1 | convolution fusion | flops 1613365248 | bytes 15990912 | tf_op jit(solution)/shard_map/while/body/dot_general | solution.py:82
  175.3 8.8 %fusion.74 = f32[128,6144]{1,0:T(8,128)S(1)} fusion(bf16[128,1024]{1,0:T(8,128)(2,1)S(1)} %get-tuple-element.387, bf16[6144,1024]{1,0:T(8,128)(2,1)} %get-tuple-element.436), kind=kOutput, calls=%fused_computation.97.clone.1 | convolution fusion | flops 1610612736 | bytes 15990784 | tf_op jit(solution)/shard_map/while/body/th,dh->td/dot_general | solution.py:95
  184.1 10.0 %fusion.75 = bf16[128,6144]{1,0:T(8,128)(2,1)} fusion(f32[128,6144]{1,0:T(8,128)S(1)} %fusion.74, bf16[128,1024]{1,0:T(8,128)(2,1)S(1)} %copy-done.3, bf16[6144,1024]{1,0:T(8,128)(2,1)} %get-tuple-element.435), kind=kOutput, calls=%fused_computation.18.clone.1 | convolution fusion | flops 1612185600 | bytes 17563648 | tf_op jit(solution)/shard_map/while/body/th,dh->td/dot_general | solution.py:100
  198.5 20.5 %convolution_add_fusion.9 = f32[1024,6144]{1,0:T(8,128)} fusion(f32[1024,6144]{1,0:T(8,128)} %get-tuple-element.410, bf16[128,1024]{1,0:T(8,128)(2,1)} %copy-done.4, bf16[128,6144]{1,0:T(8,128)(2,1)} %gather_fusion.1, pred[128]{0:T(512)(128)(4,1)S(1)} %get-tuple-element.386), kind=kOutput, calls=%fused_computation.14.clone.1 | convolution fusion | flops 1617690624 | bytes 52166784 | tf_op jit(solution)/shard_map/while/body/th,td->hd/dot_general | solution.py:108
  219.0 20.6 %convolution_add_fusion.8 = f32[6144,1024]{1,0:T(8,128)} fusion(f32[6144,1024]{1,0:T(8,128)} %get-tuple-element.409, bf16[128,1024]{1,0:T(8,128)(2,1)} %get-tuple-element.388, bf16[128,6144]{1,0:T(8,128)(2,1)} %gather_fusion, pred[128]{0:T(512)(128)(4,1)S(1)} %get-tuple-element.386), kind=kOutput, calls=%fused_computation.15.clone.1 | convolution fusion | flops 1617690624 | bytes 52166784 | tf_op jit(solution)/shard_map/while/body/td,th->dh/dot_general | solution.py:105
  239.6 16.8 %convolution_add_fusion.7 = f32[6144,1024]{1,0:T(8,128)} fusion(f32[6144,1024]{1,0:T(8,128)} %get-tuple-element.408, bf16[128,1024]{1,0:T(8,128)(2,1)S(1)} %get-tuple-element.387, bf16[128,6144]{1,0:T(8,128)(2,1)} %gather_fusion, pred[128]{0:T(512)(128)(4,1)S(1)} %get-tuple-element.386), kind=kOutput, calls=%fused_computation.16.clone.1 | convolution fusion | flops 1617690624 | bytes 52166784 | tf_op jit(solution)/shard_map/while/body/td,th->dh/dot_general | solution.py:102
  269.8 34.3 %reduce.14 = bf16[6144,128]{1,0:T(8,128)(2,1)S(1)} reduce(bf16[6144,1,128]{2,1,0:T(2,128)(2,1)} %bitcast.136, bf16[]{:T(256)} %broadcast.414), dimensions={1}, to_apply=%bitcast.78.reduce_sub_computation | reduce | bytes 3145730
  314.7 34.3 %reduce.13 = bf16[6144,128]{1,0:T(8,128)(2,1)S(1)} reduce(bf16[6144,1,128]{2,1,0:T(2,128)(2,1)} %bitcast.137, bf16[]{:T(256)} %broadcast.414), dimensions={1}, to_apply=%bitcast.76.reduce_sub_computation | reduce | bytes 3145730
  365.0 11.4 %all-to-all-done.2 = bf16[4,2,98304]{2,1,0:T(2,128)(2,1)} async-done(((bf16[4,2,98304]{2,1,0:T(2,128)(2,1)}), bf16[4,2,98304]{2,1,0:T(2,128)(2,1)}, u32[]{:S(2)}, u32[]{:S(2)}) %all-to-all-start.2) | async-done | bytes 1572896 | tf_op jit(solution)/shard_map/all_to_all | solution.py:127
  387.3 15.4 %convert_element_type.83 = bf16[6144,1024]{1,0:T(8,128)(2,1)} convert(f32[6144,1024]{1,0:T(8,128)} %get-tuple-element.199) | non-fusion elementwise | flops 6291456 | bytes 37748736 | tf_op jit(solution)/shard_map/convert_element_type | solution.py:159
  402.8 15.4 %convert_element_type.84 = bf16[6144,1024]{1,0:T(8,128)(2,1)} convert(f32[6144,1024]{1,0:T(8,128)} %get-tuple-element.200) | non-fusion elementwise | flops 6291456 | bytes 37748736 | tf_op jit(solution)/shard_map/convert_element_type | solution.py:160
  425.4 19.9 %all-reduce.5.cloned.1.call-done = (bf16[2,128,1536]{2,0,1:T(2,128)(2,1)}, bf16[2,128,1536]{2,0,1:T(2,128)(2,1)}) async-done(((bf16[2,128,1536]{2,0,1:T(2,128)(2,1)}, bf16[2,128,1536]{2,0,1:T(2,128)(2,1)}), (bf16[2,128,1536]{2,0,1:T(2,128)(2,1)}, bf16[2,128,1536]{2,0,1:T(2,128)(2,1)})) %all-reduce.5.cloned.1.call-update) | async-done | bytes 1572880
  (147 shorter events, 77.8 us)
Async XLA Ops:
  7.2 14.3 %copy-start.17 = (f32[128,2]{0,1:T(2,128)S(1)}, f32[128,2]{0,1:T(2,128)}, u32[]{:S(2)}) copy-start(f32[128,2]{0,1:T(2,128)} %param.12) | copy-start | bytes 3076
  7.2 39.1 %all-gather.3.cloned.1.call-start = ((), (), s32[]{:S(2)}) async-start(), calls=%async_computation.4 | async-start | bytes 1769472 | tf_op jit(solution)/shard_map/all_gather | solution.py:60
  9.6 13.4 %copy-start.6 = (bf16[128,1536]{1,0:T(8,128)(2,1)S(1)}, bf16[128,1536]{1,0:T(8,128)(2,1)}, u32[]{:S(2)}) copy-start(bf16[128,1536]{1,0:T(8,128)(2,1)} %param.10) | copy-start | bytes 1179652
  21.5 51.6 %all-gather.5.cloned.1.call-start = ((), (), s32[]{:S(2)}) async-start(), calls=%async_computation.5 | async-start | bytes 1769472 | tf_op jit(solution)/shard_map/all_gather | solution.py:61
  22.2 10.8 %copy-start.13 = (s32[1024,2]{0,1:T(2,128)S(1)}, s32[1024,2]{0,1:T(2,128)}, u32[]{:S(2)}) copy-start(s32[1024,2]{0,1:T(2,128)} %param.11) | copy-start | bytes 24580
  150.2 9.5 %copy-start.2 = (bf16[128,6144]{1,0:T(8,128)(2,1)S(1)}, bf16[128,6144]{1,0:T(8,128)(2,1)}, u32[]{:S(2)}) copy-start(bf16[128,6144]{1,0:T(8,128)(2,1)} %gather_fusion) | copy-start | bytes 4718596 | tf_op jit(solution)/shard_map/while
  150.2 17.8 %slice-start.6 = ((s8[12582912]{0:T(1024)(128)(4,1)}), s8[4194304]{0:T(1024)(128)(4,1)S(1)}, s32[]{:S(2)}) async-start(s8[12582912]{0:T(1024)(128)(4,1)} %bitcast.133), calls=%async_computation.13 | async-start | bytes 8388608 | tf_op jit(solution)/shard_map/while
  150.2 17.8 %slice-start.7 = ((s8[12582912]{0:T(1024)(128)(4,1)}), s8[4194304]{0:T(1024)(128)(4,1)S(1)}, s32[]{:S(2)}) async-start(s8[12582912]{0:T(1024)(128)(4,1)} %bitcast.133), calls=%async_computation.14 | async-start | bytes 8388608 | tf_op jit(solution)/shard_map/while
  159.7 8.3 %slice-start.8 = ((s8[12582912]{0:T(1024)(128)(4,1)}), s8[4194304]{0:T(1024)(128)(4,1)S(1)}, s32[]{:S(2)}) async-start(s8[12582912]{0:T(1024)(128)(4,1)} %bitcast.133), calls=%async_computation.15 | async-start | bytes 8388608 | tf_op jit(solution)/shard_map/while
  175.3 8.8 %copy-start.3 = (bf16[128,1024]{1,0:T(8,128)(2,1)S(1)}, bf16[128,1024]{1,0:T(8,128)(2,1)}, u32[]{:S(2)}) copy-start(bf16[128,1024]{1,0:T(8,128)(2,1)} %get-tuple-element.388) | copy-start | bytes 786436 | tf_op jit(solution)/shard_map/while
  305.9 44.9 %all-to-all-start.3 = ((bf16[4,2,98304]{2,1,0:T(2,128)(2,1)}), bf16[4,2,98304]{2,1,0:T(2,128)(2,1)S(1)}, u32[]{:S(2)}, u32[]{:S(2)}) async-start(bf16[4,2,98304]{2,1,0:T(2,128)(2,1)} %reshape.374), calls=%async_computation.3 | async-start | bytes 3145728 | tf_op jit(solution)/shard_map/all_to_all | solution.py:128
  350.9 5.8 %copy-start.8 = (s32[128,2]{1,0:T(8,128)S(1)}, s32[128,2]{1,0:T(8,128)}, u32[]{:S(2)}) copy-start(s32[128,2]{1,0:T(8,128)} %copy-done.7) | copy-start | bytes 3076
  350.9 5.8 %copy-start.10 = (s32[128,2]{1,0:T(8,128)S(1)}, s32[128,2]{1,0:T(8,128)}, u32[]{:S(2)}) copy-start(s32[128,2]{1,0:T(8,128)} %copy-done.9) | copy-start | bytes 3076
  352.0 24.3 %all-to-all-start.2 = ((bf16[4,2,98304]{2,1,0:T(2,128)(2,1)}), bf16[4,2,98304]{2,1,0:T(2,128)(2,1)}, u32[]{:S(2)}, u32[]{:S(2)}) async-start(bf16[4,2,98304]{2,1,0:T(2,128)(2,1)} %reshape.372), calls=%async_computation.2 | async-start | bytes 3145728 | tf_op jit(solution)/shard_map/all_to_all | solution.py:127
  356.4 89.0 %all-reduce.5.cloned.1.call-start = ((), (), s32[]{:S(2)}) async-start(), calls=%async_computation.6 | async-start | bytes 3145728
  382.7 1.9 copy-start.12
  382.7 2.8 copy-start.15
  382.7 3.0 copy-start.18
  387.3 30.9 %slice-start = ((s8[25165824]{0:T(1024)(128)(4,1)}), s8[4194304]{0:T(1024)(128)(4,1)S(1)}, s32[]{:S(2)}) async-start(s8[25165824]{0:T(1024)(128)(4,1)} %bitcast.131), calls=%async_computation.7 | async-start | bytes 8388608
  387.3 30.9 %slice-start.1 = ((s8[25165824]{0:T(1024)(128)(4,1)}), s8[4194304]{0:T(1024)(128)(4,1)S(1)}, s32[]{:S(2)}) async-start(s8[25165824]{0:T(1024)(128)(4,1)} %bitcast.131), calls=%async_computation.8 | async-start | bytes 8388608
  387.3 30.8 %slice-start.2 = ((s8[25165824]{0:T(1024)(128)(4,1)}), s8[4194304]{0:T(1024)(128)(4,1)S(1)}, s32[]{:S(2)}) async-start(s8[25165824]{0:T(1024)(128)(4,1)} %bitcast.131), calls=%async_computation.9 | async-start | bytes 8388608
  402.7 15.4 %slice-start.3 = ((s8[25165824]{0:T(1024)(128)(4,1)}), s8[4194304]{0:T(1024)(128)(4,1)S(1)}, s32[]{:S(2)}) async-start(s8[25165824]{0:T(1024)(128)(4,1)} %bitcast.131), calls=%async_computation.10 | async-start | bytes 8388608
  402.7 15.4 %slice-start.4 = ((s8[25165824]{0:T(1024)(128)(4,1)}), s8[4194304]{0:T(1024)(128)(4,1)S(1)}, s32[]{:S(2)}) async-start(s8[25165824]{0:T(1024)(128)(4,1)} %bitcast.131), calls=%async_computation.11 | async-start | bytes 8388608
  402.7 17.1 %slice-start.5 = ((s8[25165824]{0:T(1024)(128)(4,1)}), s8[4194304]{0:T(1024)(128)(4,1)S(1)}, s32[]{:S(2)}) async-start(s8[25165824]{0:T(1024)(128)(4,1)} %bitcast.131), calls=%async_computation.12 | async-start | bytes 8388608
  (9 other events, 9.0 us)
Sparse Core Ops, SparseCore 0:
  21.6 24.6 all-gather.2
  48.5 24.5 all-gather.4
  384.8 60.5 all-reduce.4
where the time goes:
time: 465 us; the launch traced here: 459 us
  other arithmetic  114 us (25%)
  matrix products  104 us (22%)
  local copies, waits for them, and re-layouts  98.2 us (21%)
  waiting for transfers between devices  69.6 us (15%)
  loops' own time  30.2 us (6%)
  blocking collectives  18.4 us (4%)
  between operations  15.8 us (3%)
  starting transfers between devices  8.35 us (2%)
    unnamed x3, other arithmetic  68.6 us
    another operation x1, loops' own time, local(): lax.fori_loop(0, tile_count, tile_step, initial)  30.2 us
    all_gather x1, waiting for transfers between devices, local(): lax.all_gather(sent_grads, 'fsdp', axis=0, tiled=True)  26.8 us
    another operation x4, local copies, waits for them, and re-layouts  23.4 us
    unnamed x58, local copies, waits for them, and re-layouts  22.2 us
    dot_general x1, matrix products, tile_step(): jnp.einsum('td,th->dh', token_tile, grad_pre_up, preferred_element_type=j...  20.6 us
    dot_general x1, matrix products, tile_step(): jnp.einsum('th,td->hd', hidden, grad_tile, preferred_element_type=jnp.flo...  20.5 us
    unnamed x4, waiting for transfers between devices  20 us
  transfers between devices with their start and end apart: 5, of which 4 were waited for; matrix products, arithmetic and copies ran while one was open for 20% of the time, Pallas kernels for 0%

commit v1 on v0

v1 whole, which is shorter than its diff:
```python
import jax
import jax.numpy as jnp
from jax import lax
from jax.experimental import pallas as pl
from jax.experimental.pallas import tpu as pltpu
from jax.sharding import PartitionSpec as P

WIN = 2
CAP = 16
VMEM_LIMIT = 56 * 1024 * 1024


def weight_grads(rows, hidden, dgate, dup):
    pieces, _, slots, width = rows.shape
    units = hidden.shape[1]
    per = 2 if units % (32 * pieces) == 0 else 1
    tile = width // per
    high = units // (pieces * per)

    def body(tok_ref, grad_ref, hid_ref, dg_ref, du_ref, og_ref, ou_ref, od_ref):
        tok = tok_ref[0, 0]
        contract = (((0,), (0,)), ((), ()))
        og_ref[...] = lax.dot_general(
            tok, dg_ref[...], contract, preferred_element_type=jnp.float32
        ).astype(jnp.bfloat16)
        ou_ref[...] = lax.dot_general(
            tok, du_ref[...], contract, preferred_element_type=jnp.float32
        ).astype(jnp.bfloat16)
        first = pl.program_id(0) * high
        hid = hid_ref[pl.ds(pl.multiple_of(first, high), high), :]
        for piece in range(pieces):
            od_ref[:, piece * width : (piece + 1) * width] = jnp.dot(
                hid, grad_ref[piece, 0], preferred_element_type=jnp.float32
            ).astype(jnp.bfloat16)

    return pl.pallas_call(
        body,
        grid=(pieces * per,),
        in_specs=[
            pl.BlockSpec((1, 1, slots, tile), lambda i: (i // per, 0, 0, i % per)),
            pl.BlockSpec((pieces, 1, slots, width), lambda i: (0, 1, 0, 0)),
            pl.BlockSpec((units, slots), lambda i: (0, 0)),
            pl.BlockSpec((slots, units), lambda i: (0, 0)),
            pl.BlockSpec((slots, units), lambda i: (0, 0)),
        ],
        out_specs=[
            pl.BlockSpec((tile, units), lambda i: (i, 0)),
            pl.BlockSpec((tile, units), lambda i: (i, 0)),
            pl.BlockSpec((high, pieces * width), lambda i: (i, 0)),
        ],
        out_shape=[
            jax.ShapeDtypeStruct((pieces * width, units), jnp.bfloat16),
            jax.ShapeDtypeStruct((pieces * width, units), jnp.bfloat16),
            jax.ShapeDtypeStruct((units, pieces * width), jnp.bfloat16),
        ],
        compiler_params=pltpu.CompilerParams(vmem_limit_bytes=VMEM_LIMIT),
        cost_estimate=pl.CostEstimate(
            flops=6 * slots * units * pieces * width,
            bytes_accessed=6 * units * pieces * width,
            transcendentals=0,
        ),
    )(rows, rows, hidden.T, dgate, dup)


def local(tokens, cotangent, routed_experts, route_weights, gate, up, down):
    pieces = lax.axis_size("expert")
    groups = lax.axis_size("fsdp")
    per_expert = pieces // WIN
    group_rows, width = tokens.shape
    slots = groups * CAP
    units = gate.shape[1]
    own_ids = lax.dynamic_slice_in_dim(
        routed_experts, lax.axis_index("fsdp") * group_rows, group_rows, 0
    )
    window = jnp.arange(WIN, dtype=jnp.int32)
    hits = own_ids[None] == window[:, None, None]
    member = jnp.any(hits, axis=2)
    weight = jnp.sum(jnp.where(hits, route_weights[None], 0.0), axis=2)
    earlier = jnp.triu(jnp.ones((group_rows, group_rows), jnp.bfloat16), 1)
    place = jnp.dot(member.astype(jnp.bfloat16), earlier, preferred_element_type=jnp.float32)
    chosen = member[:, None, :] & (
        place[:, None, :] == jnp.arange(CAP, dtype=jnp.float32)[None, :, None]
    )
    pick = chosen.astype(jnp.bfloat16).reshape(WIN * CAP, group_rows)
    slot_weight = jnp.sum(jnp.where(chosen, weight[:, None, :], 0.0), axis=2).reshape(-1, 1)
    tok_slots = jnp.dot(pick, tokens, preferred_element_type=jnp.float32).astype(jnp.bfloat16)
    cot_slots = jnp.dot(pick, cotangent, preferred_element_type=jnp.float32)
    grad_slots = (slot_weight * cot_slots).astype(jnp.bfloat16)
    sent = jnp.stack([tok_slots, grad_slots]).reshape(2, WIN, CAP, width).transpose(1, 0, 2, 3)
    sent = jnp.repeat(sent, per_expert, axis=0)
    got = lax.all_to_all(sent, "expert", split_axis=0, concat_axis=0, tiled=True)
    rows = lax.all_gather(got, "fsdp", axis=2, tiled=True)
    tok = rows[:, 0]
    grad = rows[:, 1]
    dims = (pieces, width, units)
    f32 = jnp.float32
    pre_gate = jnp.einsum("etd,edh->th", tok, gate.reshape(dims), preferred_element_type=f32)
    pre_up = jnp.einsum("etd,edh->th", tok, up.reshape(dims), preferred_element_type=f32)
    grad_flat = grad.transpose(1, 0, 2).reshape(slots, pieces * width)
    grad_hidden = jnp.einsum("td,hd->th", grad_flat, down, preferred_element_type=f32)
    sig = jax.nn.sigmoid(pre_gate)
    activated = pre_gate * sig
    hidden = (activated * pre_up).astype(jnp.bfloat16)
    dgate = (grad_hidden * pre_up * (sig * (1.0 + pre_gate * (1.0 - sig)))).astype(jnp.bfloat16)
    dup = (grad_hidden * activated).astype(jnp.bfloat16)
    out_part = jnp.dot(hidden, down, preferred_element_type=f32)
    back_part = jnp.einsum("th,dh->td", dgate, gate, preferred_element_type=f32)
    back_part = back_part + jnp.einsum("th,dh->td", dup, up, preferred_element_type=f32)
    parts = jnp.stack([out_part.astype(jnp.bfloat16), back_part.astype(jnp.bfloat16)])
    parts = parts.reshape(2, slots, pieces, width).transpose(2, 0, 1, 3)
    parts = lax.all_to_all(parts, "expert", split_axis=0, concat_axis=0, tiled=True)
    parts = jnp.sum(
        parts.reshape(WIN, per_expert, 2, groups, CAP, width).astype(f32), axis=1
    ).astype(jnp.bfloat16)
    parts = parts.transpose(2, 0, 1, 3, 4)
    parts = lax.all_to_all(parts, "fsdp", split_axis=0, concat_axis=0, tiled=True)
    total = jnp.sum(parts.astype(f32), axis=0).astype(jnp.bfloat16)
    picked = jnp.einsum(
        "kst,krsd->krtd", pick.reshape(WIN, CAP, group_rows), total, preferred_element_type=f32
    )
    layer = jnp.sum(weight[:, :, None] * picked[:, 0], axis=0).astype(jnp.bfloat16)
    back = jnp.sum(picked[:, 1], axis=0).astype(jnp.bfloat16)
    dgates, dups, ddown = weight_grads(rows, hidden, dgate, dup)
    return layer, back, dgates, dups, ddown


def solution(mesh):
    columns = P(None, ("expert", "fsdp"))
    lines = P(("expert", "fsdp"), None)
    split = P("fsdp", "expert")
    return jax.shard_map(
        local,
        mesh=mesh,
        in_specs=(split, split, P(), P("fsdp", None), columns, columns, lines),
        out_specs=(split, split, columns, columns, lines),
        check_vma=False,
    )
```

time: 465 us -> 218 us (0.47); the launches traced: 459 us -> 217 us
  other arithmetic: 114 us -> 4.72 us
  local copies, waits for them, and re-layouts: 98.2 us -> 24.7 us
  matrix products: 104 us -> 42.5 us
  blocking collectives: 18.4 us -> 52.6 us
  loops' own time: 30.2 us -> 0 us
  Pallas kernels: 0 us -> 15.6 us
  waiting for transfers between devices: 69.6 us -> 59.1 us
  starting transfers between devices: 8.35 us -> 3.62 us
    unnamed x3 -> x0, other arithmetic: 68.6 us -> none
    dot_general x9 -> x10, matrix products: 104 us -> 42.5 us  [the longest x1 8.96 us: local(): back_part = jnp.einsum('th,dh->td', dgate, gate, preferred_element_type=f32)]
    convert_element_type x7 -> x1, other arithmetic: 38.3 us -> 0.86 us  [local(): hidden = (activated * pre_up).astype(jnp.bfloat16)]
    all_to_all x2, blocking collectives: 18.4 us -> 52.6 us  [the longest x1 40.5 us: local(): lax.all_to_all(parts, 'expert', split_axis=0, concat_axis=0, tiled=True)]
    another operation x1 -> x0, loops' own time: 30.2 us -> none  [local(): lax.fori_loop(0, tile_count, tile_step, initial)]
    broadcast_in_dim x3 -> x1, local copies, waits for them, and re-layouts: 21.7 us -> 0.03 us  [local(): sent = jnp.repeat(sent, per_expert, axis=0)]
    unnamed x4 -> x1, waiting for transfers between devices: 20 us -> 0.02 us
    gather x13 -> x0, local copies, waits for them, and re-layouts: 18.3 us -> none  [the longest x1 5.75 us: tile_step(): token_tile = jnp.where(is_valid[:, None], token_rows[slot_index], bf_zero)]
  transfers between devices with their start and end apart: 5 -> 2, of which waited for: 4 -> 2; matrix products, arithmetic and copies ran while one was open for 20% -> 1% of each run, Pallas kernels for 0% -> 7%
where the time goes in v1:
time: 218 us; the launch traced here: 217 us
  waiting for transfers between devices  59.1 us (27%)
  blocking collectives  52.6 us (24%)
  matrix products  42.5 us (19%)
  local copies, waits for them, and re-layouts  24.7 us (11%)
  Pallas kernels  15.6 us (7%)
  between operations  14.3 us (7%)
  other arithmetic  4.72 us (2%)
  starting transfers between devices  3.62 us (2%)
    all_to_all x1, blocking collectives, local(): lax.all_to_all(parts, 'expert', split_axis=0, concat_axis=0, tiled=True)  40.5 us
    all_gather x1, waiting for transfers between devices, local(): rows = lax.all_gather(got, 'fsdp', axis=2, tiled=True)  38.2 us
    all_to_all x1, waiting for transfers between devices, local(): lax.all_to_all(parts, 'fsdp', split_axis=0, concat_axis=0, tiled=True)  20.9 us
    pallas_call x1, Pallas kernels, weight_grads(): pl.pallas_call(body, grid=(pieces * per,), in_specs=[pl.BlockSpec((1, 1,...  15.6 us
    all_to_all x1, blocking collectives, local(): lax.all_to_all(sent, 'expert', split_axis=0, concat_axis=0, tiled=True)  12.2 us
    unnamed x31, local copies, waits for them, and re-layouts  9.52 us
    another operation x4, local copies, waits for them, and re-layouts, local(): jnp.stack([out_part.astype(jnp.bfloat16), back_part.astype(jnp.bfloat16)])  8.99 us
    dot_general x1, matrix products, local(): back_part = jnp.einsum('th,dh->td', dgate, gate, preferred_element_type=f32)  8.96 us
  transfers between devices with their start and end apart: 2, of which 2 were waited for; matrix products, arithmetic and copies ran while one was open for 1% of the time, Pallas kernels for 7%

profile of v1, /device:TPU:0, one launch (start us, length us, event | category | flops | bytes accessed | tf_op | source)
XLA Modules:
  0.0 217.2 jit_solution(1027456753837751657)
XLA Ops:
  9.3 1.2 fusion.1
  10.6 12.2 %all_to_all.15 = bf16[4,2,16,1536]{3,2,1,0:T(8,128)(2,1)} all-to-all(bf16[4,2,16,1536]{3,2,1,0:T(8,128)(2,1)S(1)} %bitcast.86), channel_id=1, replica_groups=mesh['expert'=4,'fsdp'=8] {'expert'}, dimensions={0} | all-to-all | bytes 786432 | tf_op jit(solution)/shard_map/all_to_all | solution.py:91
  22.8 38.2 %all-gather.2.cloned.1.call-done.tok_ref.grad_ref = bf16[4,2,128,1536]{3,2,1,0:T(8,128)(2,1)} async-done(((bf16[4,2,16,1536]{3,2,1,0:T(8,128)(2,1)}), bf16[4,2,128,1536]{3,2,1,0:T(8,128)(2,1)}) %all-gather.2.cloned.1.call-update) | async-done | bytes 3145744 | tf_op jit(solution)/shard_map/all_gather | solution.py:92
  61.0 7.0 %fusion.7 = f32[128,1024]{1,0:T(8,128)S(1)} fusion(bf16[4,1536,1024]{2,1,0:T(8,128)(2,1)} %bitcast.82, bf16[4,2,128,1536]{3,2,1,0:T(8,128)(2,1)} %all-gather.2.cloned.1.call-done.tok_ref.grad_ref), kind=kOutput, calls=%fused_computation.18 | convolution fusion | flops 1610612736 | bytes 14680064 | tf_op jit(solution)/shard_map/etd,edh->th/dot_general | solution.py:98
  68.0 1.8 copy-done.2
  69.8 3.6 %fusion.6 = f32[128,1024]{1,0:T(8,128)S(1)} fusion(bf16[4,1536,1024]{2,1,0:T(8,128)(2,1)S(1)} %bitcast.81, bf16[4,2,128,1536]{3,2,1,0:T(8,128)(2,1)} %all-gather.2.cloned.1.call-done.tok_ref.grad_ref), kind=kOutput, calls=%fused_computation.17 | convolution fusion | flops 1610612736 | bytes 14680064 | tf_op jit(solution)/shard_map/etd,edh->th/dot_general | solution.py:97
  75.0 3.0 %convolution_convert_fusion = bf16[128,6144]{1,0:T(8,128)(2,1)} fusion(bf16[1024,6144]{1,0:T(8,128)(2,1)S(1)} %copy-done.3, f32[128,1024]{1,0:T(8,128)S(1)} %fusion.7, f32[128,1024]{1,0:T(8,128)S(1)} %fusion.6), kind=kOutput, calls=%fused_computation.2 | convolution fusion | flops 1612185600 | bytes 15204352 | tf_op jit(solution)/shard_map/dot_general | solution.py:106
  78.1 4.7 %stack.21 = bf16[1,128,4,1536]{3,2,1,0:T(4,128)(2,1)} reshape(bf16[128,6144]{1,0:T(8,128)(2,1)} %convolution_convert_fusion) | data formatting | bytes 3145728 | tf_op jit(solution)/shard_map/stack | solution.py:109
  82.8 2.8 %copy.37 = bf16[1,128,4,1536]{3,1,0,2:T(8,128)(2,1)} copy(bf16[1,128,4,1536]{3,2,1,0:T(4,128)(2,1)} %stack.21) | data formatting | bytes 3145728 | tf_op jit(solution)/shard_map/stack | solution.py:109
  85.6 1.2 slice_bitcast_fusion.1
  86.8 2.2 %copy.36 = bf16[128,4,1536]{0,2,1:T(8,128)(2,1)S(1)} copy(bf16[128,4,1536]{2,0,1:T(8,128)(2,1)} %slice_bitcast_fusion.1) | data formatting | bytes 3145728 | tf_op jit(solution)/shard_map/transpose | solution.py:99
  89.0 8.9 %multiply_convert_fusion = (bf16[128,1024]{1,0:T(8,128)(2,1)S(1)}, bf16[128,1024]{1,0:T(8,128)(2,1)S(1)}) fusion(f32[128,1024]{1,0:T(8,128)S(1)} %copy-done.10, f32[128,1024]{1,0:T(8,128)S(1)} %copy-done.7, bf16[128,6144]{0,1:T(8,128)(2,1)S(1)} %bitcast.85, bf16[1024,6144]{1,0:T(8,128)(2,1)} %param.13), kind=kOutput, calls=%fused_computation.26 | convolution fusion | flops 1612316672 | bytes 15728640 | tf_op jit(solution)/shard_map/td,hd->th/dot_general | solution.py:100
  98.0 9.0 %fusion.29 = f32[128,6144]{1,0:T(8,128)S(1)} fusion(bf16[128,1024]{1,0:T(8,128)(2,1)S(1)} %get-tuple-element.22.dg_ref, bf16[6144,1024]{1,0:T(8,128)(2,1)} %param.11), kind=kOutput, calls=%fused_computation.52 | convolution fusion | flops 1610612736 | bytes 15990784 | tf_op jit(solution)/shard_map/th,dh->td/dot_general | solution.py:107
  107.0 8.9 %fusion = bf16[128,6144]{1,0:T(8,128)(2,1)S(1)} fusion(f32[128,6144]{1,0:T(8,128)S(1)} %fusion.29, bf16[128,1024]{1,0:T(8,128)(2,1)S(1)} %get-tuple-element.21.du_ref, bf16[6144,1024]{1,0:T(8,128)(2,1)} %param.12), kind=kOutput, calls=%fused_computation.1 | convolution fusion | flops 1612185600 | bytes 17563648 | tf_op jit(solution)/shard_map/th,dh->td/dot_general | solution.py:108
  115.9 1.2 stack.22
  117.4 1.1 copy-done.5
  118.8 40.5 %all_to_all.16 = bf16[4,2,128,1536]{3,2,1,0:T(8,128)(2,1)S(1)} all-to-all(bf16[4,2,128,1536]{3,2,1,0:T(8,128)(2,1)S(1)} %maximum_bitcast_fusion), channel_id=1, replica_groups=mesh['expert'=4,'fsdp'=8] {'expert'}, dimensions={0} | all-to-all | bytes 6291456 | tf_op jit(solution)/shard_map/all_to_all | solution.py:111
  159.2 2.2 %reduce_sum.62 = bf16[2,2,8,16,1536]{4,3,2,1,0:T(8,128)(2,1)} reduce(bf16[2,2,2,8,16,1536]{5,4,3,2,1,0:T(8,128)(2,1)S(1)} %bitcast.83, bf16[]{:T(256)} %constant.20.clone.1), dimensions={1}, to_apply=%region_3.4 | reduce | flops 786432 | bytes 4718594 | tf_op jit(solution)/shard_map/reduce_sum | solution.py:112
  161.5 3.0 %copy.48 = bf16[2,2,8,16,1536]{4,0,3,2,1:T(2,128)(2,1)S(1)} copy(bf16[2,2,8,16,1536]{4,3,2,1,0:T(8,128)(2,1)} %reduce_sum.62) | data formatting | bytes 3145728
  164.5 1.4 copy.40
  166.0 3.6 %all-to-all-start.2 = ((bf16[8,2,2,16,1536]{4,3,2,1,0:T(8,128)(2,1)}), bf16[8,2,2,16,1536]{4,3,2,1,0:T(8,128)(2,1)S(1)}, u32[]{:S(2)}, u32[]{:S(2)}) async-start(bf16[8,2,2,16,1536]{4,3,2,1,0:T(8,128)(2,1)} %copy.40), calls=%async_computation.2 | async-start | bytes 3145728 | tf_op jit(solution)/shard_map/all_to_all | solution.py:116
  170.8 15.6 %shard_map.110 = (bf16[6144,1024]{1,0:T(8,128)(2,1)}, bf16[6144,1024]{1,0:T(8,128)(2,1)}, bf16[1024,6144]{1,0:T(8,128)(2,1)}) custom-call(bf16[4,2,128,1536]{3,2,1,0:T(8,128)(2,1)} %all-gather.2.cloned.1.call-done.tok_ref.grad_ref, bf16[4,2,128,1536]{3,2,1,0:T(8,128)(2,1)} %all-gather.2.cloned.1.call-done.tok_ref.grad_ref, bf16[1024,128]{1,0:T(8,128)(2,1)} %fusion.8.hid_ref, ...), custom_call_target="tpu_custom_call" | custom-call | flops 4831838208 | bytes 37748736 | tf_op jit(solution)/shard_map/pallas_call | solution.py:36
  186.4 20.9 %all-to-all-done.2 = bf16[8,2,2,16,1536]{4,3,2,1,0:T(8,128)(2,1)S(1)} async-done(((bf16[8,2,2,16,1536]{4,3,2,1,0:T(8,128)(2,1)}), bf16[8,2,2,16,1536]{4,3,2,1,0:T(8,128)(2,1)S(1)}, u32[]{:S(2)}, u32[]{:S(2)}) %all-to-all-start.2) | async-done | bytes 1572896 | tf_op jit(solution)/shard_map/all_to_all | solution.py:116
  208.5 0.9 copy.44
  (51 shorter events, 7.8 us)
Async XLA Ops:
  7.2 2.0 copy-start
  7.2 53.8 %all-gather.2.cloned.1.call-start = ((), (), s32[]{:S(2)}) async-start(), calls=%async_computation.3 | async-start | bytes 3538944 | tf_op jit(solution)/shard_map/all_gather | solution.py:92
  61.0 8.8 %copy-start.2 = (bf16[6144,1024]{1,0:T(8,128)(2,1)S(1)}, bf16[6144,1024]{1,0:T(8,128)(2,1)}, u32[]{:S(2)}) copy-start(bf16[6144,1024]{1,0:T(8,128)(2,1)} %param.11) | copy-start | bytes 37748740
  68.0 5.4 %copy-start.6 = (f32[128,1024]{1,0:T(8,128)}, f32[128,1024]{1,0:T(8,128)S(1)}, u32[]{:S(2)}) copy-start(f32[128,1024]{1,0:T(8,128)S(1)} %fusion.7) | copy-start | bytes 1572868
  69.8 5.2 %copy-start.3 = (bf16[1024,6144]{1,0:T(8,128)(2,1)S(1)}, bf16[1024,6144]{1,0:T(8,128)(2,1)}, u32[]{:S(2)}) copy-start(bf16[1024,6144]{1,0:T(8,128)(2,1)} %param.13) | copy-start | bytes 37748740
  73.4 0.8 copy-start.9
  78.1 7.5 %copy-start.4 = (bf16[4,2,128,1536]{3,2,1,0:T(8,128)(2,1)S(1)}, bf16[4,2,128,1536]{3,2,1,0:T(8,128)(2,1)}, u32[]{:S(2)}) copy-start(bf16[4,2,128,1536]{3,2,1,0:T(8,128)(2,1)} %all-gather.2.cloned.1.call-done.tok_ref.grad_ref) | copy-start | bytes 9437188
  86.8 2.2 %copy-start.7 = (f32[128,1024]{1,0:T(8,128)S(1)}, f32[128,1024]{1,0:T(8,128)}, u32[]{:S(2)}) copy-start(f32[128,1024]{1,0:T(8,128)} %copy-done.6) | copy-start | bytes 1572868
  86.8 2.2 %copy-start.10 = (f32[128,1024]{1,0:T(8,128)S(1)}, f32[128,1024]{1,0:T(8,128)}, u32[]{:S(2)}) copy-start(f32[128,1024]{1,0:T(8,128)} %copy-done.9) | copy-start | bytes 1572868
  98.0 9.0 %copy-start.13 = (bf16[128,1024]{1,0:T(8,128)(2,1)}, bf16[128,1024]{1,0:T(8,128)(2,1)S(1)}, u32[]{:S(2)}) copy-start(bf16[128,1024]{1,0:T(8,128)(2,1)S(1)} %get-tuple-element.22.dg_ref) | copy-start | bytes 786436
  98.0 9.0 %copy-start.12 = (bf16[128,1024]{1,0:T(8,128)(2,1)}, bf16[128,1024]{1,0:T(8,128)(2,1)S(1)}, u32[]{:S(2)}) copy-start(bf16[128,1024]{1,0:T(8,128)(2,1)S(1)} %get-tuple-element.21.du_ref) | copy-start | bytes 786436
  117.1 1.4 copy-start.5
  164.5 5.0 %copy-start.11 = (f32[128,1024]{1,0:T(8,128)S(1)}, f32[128,1024]{1,0:T(8,128)}, u32[]{:S(2)}) copy-start(f32[128,1024]{1,0:T(8,128)} %copy-done.9) | copy-start | bytes 1572868
  164.5 5.2 %copy-start.8 = (f32[128,1024]{1,0:T(8,128)S(1)}, f32[128,1024]{1,0:T(8,128)}, u32[]{:S(2)}) copy-start(f32[128,1024]{1,0:T(8,128)} %copy-done.6) | copy-start | bytes 1572868
  166.0 41.3 %all-to-all-start.2 = ((bf16[8,2,2,16,1536]{4,3,2,1,0:T(8,128)(2,1)}), bf16[8,2,2,16,1536]{4,3,2,1,0:T(8,128)(2,1)S(1)}, u32[]{:S(2)}, u32[]{:S(2)}) async-start(bf16[8,2,2,16,1536]{4,3,2,1,0:T(8,128)(2,1)} %copy.40), calls=%async_computation.2 | async-start | bytes 3145728 | tf_op jit(solution)/shard_map/all_to_all | solution.py:116
  207.5 2.8 %copy-start.1 = (bf16[128,1536]{1,0:T(8,128)(2,1)S(1)}, bf16[128,1536]{1,0:T(8,128)(2,1)}, u32[]{:S(2)}) copy-start(bf16[128,1536]{1,0:T(8,128)(2,1)} %param.7) | copy-start | bytes 1179652
Sparse Core Ops, SparseCore 0:
  22.9 37.9 all-gather.1

commit v2 on v1

--- a/solution.py
+++ b/solution.py
@@ -62,13 +62,269 @@
     )(rows, rows, hidden.T, dgate, dup)
 
 
-def local(tokens, cotangent, routed_experts, route_weights, gate, up, down):
+def exchange_and_products(pick, slot_weight, weight, tokens, cotangent, gate, up, down):
     pieces = lax.axis_size("expert")
     groups = lax.axis_size("fsdp")
     per_expert = pieces // WIN
+    depth = groups // 2
     group_rows, width = tokens.shape
     slots = groups * CAP
+    half = slots // 2
     units = gate.shape[1]
+    bf16, f32 = jnp.bfloat16, jnp.float32
+    unit_tile = min(256, units)
+    col_tile = 512 if width % 512 == 0 else 256
+    n_copies = (depth - 1) + depth * (pieces - 1) + depth * pieces + pieces + (pieces - 1) + (depth - 1)
+    rows_t = (((0,), (0,)), ((), ()))
+    cols_t = (((1,), (1,)), ((), ()))
+
+    def body(
+        pick_ref, sw_ref, w_ref, tok_ref, cot_ref, gate_hbm, up_hbm, down_hbm,
+        layer_ref, back_ref, hid_ref, dg_ref, du_ref, rows_out,
+        gate_v, up_v, down_v, held, rows, parts, paired, spread, summed, landed,
+        load_sem, send_sem, recv_sem,
+    ):
+        e = lax.axis_index("expert")
+        f = lax.axis_index("fsdp")
+        z = f // 2
+        c = lax.rem(f, 2)
+        own = e // per_expert
+        counter = [0]
+        started = []
+
+        def send(src, dst, to_e, to_f):
+            at = counter[0]
+            counter[0] += 1
+            copy = pltpu.make_async_remote_copy(
+                src_ref=src,
+                dst_ref=dst,
+                send_sem=send_sem.at[at],
+                recv_sem=recv_sem.at[at],
+                device_id={"expert": to_e, "fsdp": to_f},
+                device_id_type=pl.DeviceIdType.MESH,
+            )
+            copy.start()
+            started.append(copy)
+            return copy
+
+        def other_e(i):
+            return lax.rem(e + i, pieces)
+
+        def other_z(j):
+            return lax.rem(z + j, depth)
+
+        barrier = pltpu.get_barrier_semaphore()
+        partners = [(e, other_z(j) * 2 + c) for j in range(1, depth)]
+        partners += [(other_e(i), f) for i in range(1, pieces)]
+        partners += [(e, z * 2 + 1 - c)]
+        for to_e, to_f in partners:
+            pl.semaphore_signal(
+                barrier,
+                inc=1,
+                device_id={"expert": to_e, "fsdp": to_f},
+                device_id_type=pl.DeviceIdType.MESH,
+            )
+
+        loads = []
+        for which, (src, dst) in enumerate(((gate_hbm, gate_v), (up_hbm, up_v), (down_hbm, down_v))):
+            step = src.shape[0] // pieces
+            for piece in range(pieces):
+                span = pl.ds(piece * step, step)
+                load = pltpu.make_async_copy(
+                    src.at[span], dst.at[span], load_sem.at[which * pieces + piece]
+                )
+                load.start()
+                loads.append(load)
+
+        tok_slots = jnp.dot(pick_ref[...], tok_ref[...], preferred_element_type=f32).astype(bf16)
+        cot_slots = jnp.dot(pick_ref[...], cot_ref[...], preferred_element_type=f32)
+        grad_slots = (sw_ref[...] * cot_slots).astype(bf16)
+        for k in range(WIN):
+            held[z, k, 0] = tok_slots[k * CAP : (k + 1) * CAP]
+            held[z, k, 1] = grad_slots[k * CAP : (k + 1) * CAP]
+        pl.semaphore_wait(barrier, len(partners))
+
+        along = [
+            send(held.at[z], held.at[z], e, other_z(j) * 2 + c) for j in range(1, depth)
+        ]
+        across = {}
+        beside = []
+
+        def place(zs):
+            return pl.ds(pl.multiple_of((c * depth + zs) * CAP, CAP), CAP)
+
+        def pass_on(j):
+            zs = lax.rem(z - j + depth, depth)
+            for i in range(pieces):
+                if i > 0:
+                    across[j, i].wait_recv()
+                came = lax.rem(e - i + pieces, pieces)
+                spot = rows.at[came, :, place(zs), :]
+                beside.append(send(spot, spot, e, z * 2 + 1 - c))
+
+        for j in range(depth):
+            zs = lax.rem(z - j + depth, depth)
+            if j > 0:
+                along[j - 1].wait_recv()
+            for i in range(1, pieces):
+                to_e = other_e(i)
+                across[j, i] = send(
+                    held.at[zs, to_e // per_expert], rows.at[e, :, place(zs), :], to_e, f
+                )
+            rows[e, :, place(zs), :] = held[zs, own]
+            if j > 0:
+                pass_on(j - 1)
+        pass_on(depth - 1)
+        for copy in beside:
+            copy.wait_recv()
+        keep = pltpu.make_async_copy(rows, rows_out, load_sem.at[3 * pieces])
+        keep.start()
+        for load in loads:
+            load.wait()
+
+        def forward(t, carry):
+            span = pl.ds(pl.multiple_of(t * unit_tile, unit_tile), unit_tile)
+            pre_gate = pre_up = grad_hidden = 0.0
+            for piece in range(pieces):
+                cols = slice(piece * width, (piece + 1) * width)
+                tok = rows[piece, 0]
+                pre_gate += jnp.dot(tok, gate_v[cols, span], preferred_element_type=f32)
+                pre_up += jnp.dot(tok, up_v[cols, span], preferred_element_type=f32)
+                grad_hidden += lax.dot_general(
+                    rows[piece, 1], down_v[span, cols], cols_t, preferred_element_type=f32
+                )
+            sig = jax.nn.sigmoid(pre_gate)
+            activated = pre_gate * sig
+            hid_ref[:, span] = (activated * pre_up).astype(bf16)
+            dg_ref[:, span] = (
+                grad_hidden * pre_up * (sig * (1.0 + pre_gate * (1.0 - sig)))
+            ).astype(bf16)
+            du_ref[:, span] = (grad_hidden * activated).astype(bf16)
+            return carry
+
+        lax.fori_loop(0, units // unit_tile, forward, 0)
+
+        mine = pl.ds(pl.multiple_of(c * half, CAP), half)
+        theirs = pl.ds(pl.multiple_of((1 - c) * half, CAP), half)
+        pairs = []
+        spreads = []
+
+        def finish(i):
+            to_e = other_e(i + 1)
+            pairs[i].wait_recv()
+            both = parts[to_e, :, mine, :].astype(f32) + paired[to_e].astype(f32)
+            if i < pieces - 1:
+                parts[to_e, :, mine, :] = both.astype(bf16)
+                spreads.append(send(parts.at[to_e, :, mine, :], spread.at[e], to_e, f))
+            else:
+                spread[e] = both.astype(bf16)
+
+        for i in range(pieces):
+            to_e = other_e(i + 1)
+
+            def backward(t, carry):
+                spot = pl.ds(pl.multiple_of(t * col_tile, col_tile), col_tile)
+                cols = pl.ds(pl.multiple_of(to_e * width + t * col_tile, 128), col_tile)
+                parts[to_e, 0, :, spot] = jnp.dot(
+                    hid_ref[...], down_v[:, cols], preferred_element_type=f32
+                ).astype(bf16)
+                back = lax.dot_general(
+                    dg_ref[...], gate_v[cols, :], cols_t, preferred_element_type=f32
+                )
+                back += lax.dot_general(
+                    du_ref[...], up_v[cols, :], cols_t, preferred_element_type=f32
+                )
+                parts[to_e, 1, :, spot] = back.astype(bf16)
+                return carry
+
+            lax.fori_loop(0, width // col_tile, backward, 0)
+            pairs.append(
+                send(parts.at[to_e, :, theirs, :], paired.at[to_e], e, z * 2 + 1 - c)
+            )
+            if i > 0:
+                finish(i - 1)
+        finish(pieces - 1)
+        for copy in spreads:
+            copy.wait_recv()
+
+        returns = []
+        for j in list(range(1, depth)) + [0]:
+            to_z = other_z(j)
+            span = pl.ds(pl.multiple_of(to_z * CAP, CAP), CAP)
+            for k in range(WIN):
+                total = 0.0
+                for piece in range(k * per_expert, (k + 1) * per_expert):
+                    total += spread[piece, :, span, :].astype(f32)
+                if j > 0:
+                    summed[j, k] = total.astype(bf16)
+                else:
+                    landed[z, k] = total.astype(bf16)
+            if j > 0:
+                returns.append(send(summed.at[j], landed.at[z], e, to_z * 2 + c))
+        for copy in returns:
+            copy.wait_recv()
+
+        layer = jnp.zeros((group_rows, width), f32)
+        back = jnp.zeros((group_rows, width), f32)
+        for k in range(WIN):
+            total = 0.0
+            for zs in range(depth):
+                total += landed[zs, k].astype(f32)
+            total = total.astype(bf16)
+            choice = pick_ref[k * CAP : (k + 1) * CAP, :]
+            layer += w_ref[:, k : k + 1] * lax.dot_general(
+                choice, total[0], rows_t, preferred_element_type=f32
+            )
+            back += lax.dot_general(choice, total[1], rows_t, preferred_element_type=f32)
+        layer_ref[...] = layer.astype(bf16)
+        back_ref[...] = back.astype(bf16)
+        for copy in started:
+            copy.wait_send()
+        keep.wait()
+
+    vmem = pl.BlockSpec(memory_space=pltpu.VMEM)
+    anywhere = pl.BlockSpec(memory_space=pl.ANY)
+    shape = jax.ShapeDtypeStruct
+    return pl.pallas_call(
+        body,
+        in_specs=[vmem] * 5 + [anywhere] * 3,
+        out_specs=[vmem] * 5 + [anywhere],
+        out_shape=[
+            shape((group_rows, width), bf16),
+            shape((group_rows, width), bf16),
+            shape((slots, units), bf16),
+            shape((slots, units), bf16),
+            shape((slots, units), bf16),
+            shape((pieces, 2, slots, width), bf16),
+        ],
+        scratch_shapes=[
+            pltpu.VMEM(gate.shape, bf16),
+            pltpu.VMEM(up.shape, bf16),
+            pltpu.VMEM(down.shape, bf16),
+            pltpu.VMEM((depth, WIN, 2, CAP, width), bf16),
+            pltpu.VMEM((pieces, 2, slots, width), bf16),
+            pltpu.VMEM((pieces, 2, slots, width), bf16),
+            pltpu.VMEM((pieces, 2, half, width), bf16),
+            pltpu.VMEM((pieces, 2, half, width), bf16),
+            pltpu.VMEM((depth, WIN, 2, CAP, width), bf16),
+            pltpu.VMEM((depth, WIN, 2, CAP, width), bf16),
+            pltpu.SemaphoreType.DMA((3 * pieces + 1,)),
+            pltpu.SemaphoreType.DMA((n_copies,)),
+            pltpu.SemaphoreType.DMA((n_copies,)),
+        ],
+        compiler_params=pltpu.CompilerParams(
+            collective_id=0, has_side_effects=True, vmem_limit_bytes=62 * 1024 * 1024
+        ),
+        cost_estimate=pl.CostEstimate(
+            flops=12 * slots * units * pieces * width,
+            bytes_accessed=6 * units * pieces * width,
+            transcendentals=slots * units,
+        ),
+    )(pick, slot_weight, weight, tokens, cotangent, gate, up, down)
+
+
+def local(tokens, cotangent, routed_experts, route_weights, gate, up, down):
+    group_rows = tokens.shape[0]
     own_ids = lax.dynamic_slice_in_dim(
         routed_experts, lax.axis_index("fsdp") * group_rows, group_rows, 0
     )
@@ -83,43 +339,9 @@
     )
     pick = chosen.astype(jnp.bfloat16).reshape(WIN * CAP, group_rows)
     slot_weight = jnp.sum(jnp.where(chosen, weight[:, None, :], 0.0), axis=2).reshape(-1, 1)
-    tok_slots = jnp.dot(pick, tokens, preferred_element_type=jnp.float32).astype(jnp.bfloat16)
-    cot_slots = jnp.dot(pick, cotangent, preferred_element_type=jnp.float32)
-    grad_slots = (slot_weight * cot_slots).astype(jnp.bfloat16)
-    sent = jnp.stack([tok_slots, grad_slots]).reshape(2, WIN, CAP, width).transpose(1, 0, 2, 3)
-    sent = jnp.repeat(sent, per_expert, axis=0)
-    got = lax.all_to_all(sent, "expert", split_axis=0, concat_axis=0, tiled=True)
-    rows = lax.all_gather(got, "fsdp", axis=2, tiled=True)
-    tok = rows[:, 0]
-    grad = rows[:, 1]
-    dims = (pieces, width, units)
-    f32 = jnp.float32
-    pre_gate = jnp.einsum("etd,edh->th", tok, gate.reshape(dims), preferred_element_type=f32)
-    pre_up = jnp.einsum("etd,edh->th", tok, up.reshape(dims), preferred_element_type=f32)
-    grad_flat = grad.transpose(1, 0, 2).reshape(slots, pieces * width)
-    grad_hidden = jnp.einsum("td,hd->th", grad_flat, down, preferred_element_type=f32)
-    sig = jax.nn.sigmoid(pre_gate)
-    activated = pre_gate * sig
-    hidden = (activated * pre_up).astype(jnp.bfloat16)
-    dgate = (grad_hidden * pre_up * (sig * (1.0 + pre_gate * (1.0 - sig)))).astype(jnp.bfloat16)
-    dup = (grad_hidden * activated).astype(jnp.bfloat16)
-    out_part = jnp.dot(hidden, down, preferred_element_type=f32)
-    back_part = jnp.einsum("th,dh->td", dgate, gate, preferred_element_type=f32)
-    back_part = back_part + jnp.einsum("th,dh->td", dup, up, preferred_element_type=f32)
-    parts = jnp.stack([out_part.astype(jnp.bfloat16), back_part.astype(jnp.bfloat16)])
-    parts = parts.reshape(2, slots, pieces, width).transpose(2, 0, 1, 3)
-    parts = lax.all_to_all(parts, "expert", split_axis=0, concat_axis=0, tiled=True)
-    parts = jnp.sum(
-        parts.reshape(WIN, per_expert, 2, groups, CAP, width).astype(f32), axis=1
-    ).astype(jnp.bfloat16)
-    parts = parts.transpose(2, 0, 1, 3, 4)
-    parts = lax.all_to_all(parts, "fsdp", split_axis=0, concat_axis=0, tiled=True)
-    total = jnp.sum(parts.astype(f32), axis=0).astype(jnp.bfloat16)
-    picked = jnp.einsum(
-        "kst,krsd->krtd", pick.reshape(WIN, CAP, group_rows), total, preferred_element_type=f32
+    layer, back, hidden, dgate, dup, rows = exchange_and_products(
+        pick, slot_weight, weight.T, tokens, cotangent, gate, up, down
     )
-    layer = jnp.sum(weight[:, :, None] * picked[:, 0], axis=0).astype(jnp.bfloat16)
-    back = jnp.sum(picked[:, 1], axis=0).astype(jnp.bfloat16)
     dgates, dups, ddown = weight_grads(rows, hidden, dgate, dup)
     return layer, back, dgates, dups, ddown
 

time: 218 us -> 111 us (0.51)
  the two profiles are of different devices: /device:TPU:0 before, /device:TPU:11 now
where the time goes in v2:
time: 111 us
  Pallas kernels  103 us (93%)
  local copies, waits for them, and re-layouts  5.58 us (5%)
  other arithmetic  1.5 us (1%)
    pallas_call x1, Pallas kernels, exchange_and_products(): pl.pallas_call(body, in_specs=[vmem] * 5 + [anywhere] * 3, out_specs=[vme...  87.1 us
    pallas_call x1, Pallas kernels, weight_grads(): pl.pallas_call(body, grid=(pieces * per,), in_specs=[pl.BlockSpec((1, 1,...  15.6 us

profile of v2, /device:TPU:11, one launch (start us, length us, event | category | flops | bytes accessed | tf_op | source)
XLA Modules:
  0.0 110.6 jit_solution(2100942813380191203)
XLA Ops:
  0.6 0.0 copy-start
  0.7 0.7 copy-done
  1.4 0.7 select_reduce_fusion.1
  2.1 0.1 fusion.1
  2.2 0.1 select_reduce_fusion
  2.3 0.1 eq.43
  2.4 0.7 fusion.7.pick_ref
  3.1 0.7 reshape.23.sw_ref
  3.8 0.7 copy.17
  4.5 0.0 copy-start.1
  4.5 87.1 %shard_map.110 = (bf16[128,1536]{1,0:T(8,128)(2,1)}, bf16[128,1536]{1,0:T(8,128)(2,1)}, bf16[128,1024]{1,0:T(8,128)(2,1)}, bf16[128,1024]{1,0:T(8,128)(2,1)}, bf...) custom-call(bf16[32,128]{1,0:T(8,128)(2,1)} %fusion.7.pick_ref, f32[32,1]{1,0:T(8,128)} %reshape.23.sw_ref, ...), custom_call_target="tpu_custom_call" | custom-call | flops 9663676416 | bytes 37748736 | tf_op jit(solution)/shard_map/pallas_call | solution.py:288
  91.6 0.0 copy-start.3
  91.6 0.0 copy-start.2
  91.6 1.9 %copy.19 = bf16[128,1024]{0,1:T(8,128)(2,1)} copy(bf16[128,1024]{1,0:T(8,128)(2,1)} %get-tuple-element.17) | data formatting | bytes 524288 | tf_op jit(solution)/shard_map/pallas_call | solution.py:288
  93.5 15.6 %shard_map.111 = (bf16[6144,1024]{1,0:T(8,128)(2,1)}, bf16[6144,1024]{1,0:T(8,128)(2,1)}, bf16[1024,6144]{1,0:T(8,128)(2,1)}) custom-call(bf16[4,2,128,1536]{3,2,1,0:T(8,128)(2,1)} %get-tuple-element.16.tok_ref.grad_ref, bf16[4,2,128,1536]{3,2,1,0:T(8,128)(2,1)} %get-tuple-element.16.tok_ref.grad_ref, bf16[1024,128]{1,0:T(8,128)(2,1)} %bitcast.12, ...), custom_call_target="tpu_custom_call" | custom-call | flops 4831838208 | bytes 37748736 | tf_op jit(solution)/shard_map/pallas_call | solution.py:36
  109.1 0.0 copy-done.3
  109.1 0.7 copy.22
  109.8 0.0 copy-done.2
  109.8 0.7 copy.23
  110.6 0.0 copy-done.1
  (3 shorter events, 0.0 us)
Async XLA Ops:
  0.6 0.7 copy-start
  4.5 106.1 %copy-start.1 = (s32[1024,2]{0,1:T(2,128)S(1)}, s32[1024,2]{0,1:T(2,128)}, u32[]{:S(2)}) copy-start(s32[1024,2]{0,1:T(2,128)} %param.9) | copy-start | bytes 24580
  91.6 17.5 %copy-start.3 = (bf16[128,1536]{1,0:T(8,128)(2,1)S(1)}, bf16[128,1536]{1,0:T(8,128)(2,1)}, u32[]{:S(2)}) copy-start(bf16[128,1536]{1,0:T(8,128)(2,1)} %get-tuple-element.28) | copy-start | bytes 1179652
  91.6 18.2 %copy-start.2 = (bf16[128,1536]{1,0:T(8,128)(2,1)S(1)}, bf16[128,1536]{1,0:T(8,128)(2,1)}, u32[]{:S(2)}) copy-start(bf16[128,1536]{1,0:T(8,128)(2,1)} %get-tuple-element.29) | copy-start | bytes 1179652

commit v3 on v2

--- a/solution.py
+++ b/solution.py
@@ -10,10 +10,10 @@
 VMEM_LIMIT = 56 * 1024 * 1024
 
 
-def weight_grads(rows, hidden, dgate, dup):
+def weight_grads(rows, hidden_t, dgate, dup):
     pieces, _, slots, width = rows.shape
-    units = hidden.shape[1]
-    per = 2 if units % (32 * pieces) == 0 else 1
+    units = dgate.shape[1]
+    per = 4 if units % (64 * pieces) == 0 and width % 512 == 0 else 1
     tile = width // per
     high = units // (pieces * per)
 
@@ -59,10 +59,10 @@
             bytes_accessed=6 * units * pieces * width,
             transcendentals=0,
         ),
-    )(rows, rows, hidden.T, dgate, dup)
-
-
-def exchange_and_products(pick, slot_weight, weight, tokens, cotangent, gate, up, down):
+    )(rows, rows, hidden_t, dgate, dup)
+
+
+def exchange_and_products(pick, ids, weights, tokens, cotangent, gate, up, down):
     pieces = lax.axis_size("expert")
     groups = lax.axis_size("fsdp")
     per_expert = pieces // WIN
@@ -74,14 +74,14 @@
     bf16, f32 = jnp.bfloat16, jnp.float32
     unit_tile = min(256, units)
     col_tile = 512 if width % 512 == 0 else 256
-    n_copies = (depth - 1) + depth * (pieces - 1) + depth * pieces + pieces + (pieces - 1) + (depth - 1)
+    n_copies = (depth - 1) + depth * (pieces - 1) + depth * pieces + pieces + depth * (pieces - 1) + (depth - 1)
     rows_t = (((0,), (0,)), ((), ()))
     cols_t = (((1,), (1,)), ((), ()))
 
     def body(
-        pick_ref, sw_ref, w_ref, tok_ref, cot_ref, gate_hbm, up_hbm, down_hbm,
-        layer_ref, back_ref, hid_ref, dg_ref, du_ref, rows_out,
-        gate_v, up_v, down_v, held, rows, parts, paired, spread, summed, landed,
+        pick_ref, ids_ref, w_ref, tok_ref, cot_ref, gate_hbm, up_hbm, down_hbm,
+        layer_ref, back_ref, hidt_ref, dg_ref, du_ref, rows_out,
+        gate_v, up_v, down_v, held, rows, parts, paired, spread, summed, landed, hid_ref, sums,
         load_sem, send_sem, recv_sem,
     ):
         e = lax.axis_index("expert")
@@ -137,11 +137,18 @@
                 loads.append(load)
 
         tok_slots = jnp.dot(pick_ref[...], tok_ref[...], preferred_element_type=f32).astype(bf16)
-        cot_slots = jnp.dot(pick_ref[...], cot_ref[...], preferred_element_type=f32)
-        grad_slots = (sw_ref[...] * cot_slots).astype(bf16)
+        cot = cot_ref[...].astype(f32)
+        row_weight = [
+            jnp.sum(jnp.where(ids_ref[...] == k, w_ref[...], 0.0), axis=1, keepdims=True)
+            for k in range(WIN)
+        ]
         for k in range(WIN):
             held[z, k, 0] = tok_slots[k * CAP : (k + 1) * CAP]
-            held[z, k, 1] = grad_slots[k * CAP : (k + 1) * CAP]
+            held[z, k, 1] = jnp.dot(
+                pick_ref[k * CAP : (k + 1) * CAP, :],
+                (row_weight[k] * cot).astype(bf16),
+                preferred_element_type=f32,
+            ).astype(bf16)
         pl.semaphore_wait(barrier, len(partners))
 
         along = [
@@ -150,16 +157,36 @@
         across = {}
         beside = []
 
+        own_beside = []
+
+        def came_from(i):
+            return lax.rem(e - i + pieces, pieces)
+
+        def products(piece, span):
+            lines = pl.ds(pl.multiple_of(piece * width, 128), width)
+            tok = rows[piece, 0]
+            return (
+                jnp.dot(tok, gate_v[lines, span], preferred_element_type=f32),
+                jnp.dot(tok, up_v[lines, span], preferred_element_type=f32),
+                lax.dot_general(
+                    rows[piece, 1], down_v[span, lines], cols_t, preferred_element_type=f32
+                ),
+            )
+
+        def first(t, carry):
+            span = pl.ds(pl.multiple_of(t * unit_tile, unit_tile), unit_tile)
+            for at, term in enumerate(products(e, span)):
+                sums[at, :, span] = term
+            return carry
+
         def place(zs):
             return pl.ds(pl.multiple_of((c * depth + zs) * CAP, CAP), CAP)
 
         def pass_on(j):
             zs = lax.rem(z - j + depth, depth)
-            for i in range(pieces):
-                if i > 0:
-                    across[j, i].wait_recv()
-                came = lax.rem(e - i + pieces, pieces)
-                spot = rows.at[came, :, place(zs), :]
+            for i in range(1, pieces):
+                across[j, i].wait_recv()
+                spot = rows.at[came_from(i), :, place(zs), :]
                 beside.append(send(spot, spot, e, z * 2 + 1 - c))
 
         for j in range(depth):
@@ -172,30 +199,34 @@
                     held.at[zs, to_e // per_expert], rows.at[e, :, place(zs), :], to_e, f
                 )
             rows[e, :, place(zs), :] = held[zs, own]
+            spot = rows.at[e, :, place(zs), :]
+            own_beside.append(send(spot, spot, e, z * 2 + 1 - c))
             if j > 0:
                 pass_on(j - 1)
+        for load in loads:
+            load.wait()
+        for copy in own_beside:
+            copy.wait_recv()
+        lax.fori_loop(0, units // unit_tile, first, 0)
         pass_on(depth - 1)
         for copy in beside:
             copy.wait_recv()
         keep = pltpu.make_async_copy(rows, rows_out, load_sem.at[3 * pieces])
         keep.start()
-        for load in loads:
-            load.wait()
 
         def forward(t, carry):
             span = pl.ds(pl.multiple_of(t * unit_tile, unit_tile), unit_tile)
-            pre_gate = pre_up = grad_hidden = 0.0
-            for piece in range(pieces):
-                cols = slice(piece * width, (piece + 1) * width)
-                tok = rows[piece, 0]
-                pre_gate += jnp.dot(tok, gate_v[cols, span], preferred_element_type=f32)
-                pre_up += jnp.dot(tok, up_v[cols, span], preferred_element_type=f32)
-                grad_hidden += lax.dot_general(
-                    rows[piece, 1], down_v[span, cols], cols_t, preferred_element_type=f32
-                )
+            pre_gate, pre_up, grad_hidden = (sums[at, :, span] for at in range(3))
+            for i in range(1, pieces):
+                more = products(came_from(i), span)
+                pre_gate += more[0]
+                pre_up += more[1]
+                grad_hidden += more[2]
             sig = jax.nn.sigmoid(pre_gate)
             activated = pre_gate * sig
-            hid_ref[:, span] = (activated * pre_up).astype(bf16)
+            hid = activated * pre_up
+            hid_ref[:, span] = hid.astype(bf16)
+            hidt_ref[span, :] = hid.T.astype(bf16)
             dg_ref[:, span] = (
                 grad_hidden * pre_up * (sig * (1.0 + pre_gate * (1.0 - sig)))
             ).astype(bf16)
@@ -207,7 +238,19 @@
         mine = pl.ds(pl.multiple_of(c * half, CAP), half)
         theirs = pl.ds(pl.multiple_of((1 - c) * half, CAP), half)
         pairs = []
-        spreads = []
+        spreads = {}
+        early = list(range(1, depth // 2 + 1))
+        late = [j for j in range(depth) if j not in early and j > 0] + [0]
+
+        def spread_out(i, j):
+            to_e = other_e(i + 1)
+            to_z = other_z(j)
+            spreads[i, j] = send(
+                parts.at[to_e, :, place(to_z), :],
+                spread.at[e, :, pl.ds(pl.multiple_of(to_z * CAP, CAP), CAP), :],
+                to_e,
+                f,
+            )
 
         def finish(i):
             to_e = other_e(i + 1)
@@ -215,7 +258,8 @@
             both = parts[to_e, :, mine, :].astype(f32) + paired[to_e].astype(f32)
             if i < pieces - 1:
                 parts[to_e, :, mine, :] = both.astype(bf16)
-                spreads.append(send(parts.at[to_e, :, mine, :], spread.at[e], to_e, f))
+                for j in early:
+                    spread_out(i, j)
             else:
                 spread[e] = both.astype(bf16)
 
@@ -244,11 +288,14 @@
             if i > 0:
                 finish(i - 1)
         finish(pieces - 1)
-        for copy in spreads:
-            copy.wait_recv()
+        for j in late:
+            for i in range(pieces - 1):
+                spread_out(i, j)
 
         returns = []
-        for j in list(range(1, depth)) + [0]:
+        for j in early + late:
+            for i in range(pieces - 1):
+                spreads[i, j].wait_recv()
             to_z = other_z(j)
             span = pl.ds(pl.multiple_of(to_z * CAP, CAP), CAP)
             for k in range(WIN):
@@ -272,7 +319,7 @@
                 total += landed[zs, k].astype(f32)
             total = total.astype(bf16)
             choice = pick_ref[k * CAP : (k + 1) * CAP, :]
-            layer += w_ref[:, k : k + 1] * lax.dot_general(
+            layer += row_weight[k] * lax.dot_general(
                 choice, total[0], rows_t, preferred_element_type=f32
             )
             back += lax.dot_general(choice, total[1], rows_t, preferred_element_type=f32)
@@ -292,7 +339,7 @@
         out_shape=[
             shape((group_rows, width), bf16),
             shape((group_rows, width), bf16),
-            shape((slots, units), bf16),
+            shape((units, slots), bf16),
             shape((slots, units), bf16),
             shape((slots, units), bf16),
             shape((pieces, 2, slots, width), bf16),
@@ -308,6 +355,8 @@
             pltpu.VMEM((pieces, 2, half, width), bf16),
             pltpu.VMEM((depth, WIN, 2, CAP, width), bf16),
             pltpu.VMEM((depth, WIN, 2, CAP, width), bf16),
+            pltpu.VMEM((slots, units), bf16),
+            pltpu.VMEM((3, slots, units), f32),
             pltpu.SemaphoreType.DMA((3 * pieces + 1,)),
             pltpu.SemaphoreType.DMA((n_copies,)),
             pltpu.SemaphoreType.DMA((n_copies,)),
@@ -320,7 +369,7 @@
             bytes_accessed=6 * units * pieces * width,
             transcendentals=slots * units,
         ),
-    )(pick, slot_weight, weight, tokens, cotangent, gate, up, down)
+    )(pick, ids, weights, tokens, cotangent, gate, up, down)
 
 
 def local(tokens, cotangent, routed_experts, route_weights, gate, up, down):
@@ -331,18 +380,16 @@
     window = jnp.arange(WIN, dtype=jnp.int32)
     hits = own_ids[None] == window[:, None, None]
     member = jnp.any(hits, axis=2)
-    weight = jnp.sum(jnp.where(hits, route_weights[None], 0.0), axis=2)
     earlier = jnp.triu(jnp.ones((group_rows, group_rows), jnp.bfloat16), 1)
     place = jnp.dot(member.astype(jnp.bfloat16), earlier, preferred_element_type=jnp.float32)
     chosen = member[:, None, :] & (
         place[:, None, :] == jnp.arange(CAP, dtype=jnp.float32)[None, :, None]
     )
     pick = chosen.astype(jnp.bfloat16).reshape(WIN * CAP, group_rows)
-    slot_weight = jnp.sum(jnp.where(chosen, weight[:, None, :], 0.0), axis=2).reshape(-1, 1)
-    layer, back, hidden, dgate, dup, rows = exchange_and_products(
-        pick, slot_weight, weight.T, tokens, cotangent, gate, up, down
+    layer, back, hidden_t, dgate, dup, rows = exchange_and_products(
+        pick, own_ids, route_weights, tokens, cotangent, gate, up, down
     )
-    dgates, dups, ddown = weight_grads(rows, hidden, dgate, dup)
+    dgates, dups, ddown = weight_grads(rows, hidden_t, dgate, dup)
     return layer, back, dgates, dups, ddown
 
 

time: 111 us -> 103 us (0.928)
  Pallas kernels: 103 us -> 96.2 us
  local copies, waits for them, and re-layouts: 5.58 us -> 4.44 us
    pallas_call x1, Pallas kernels: 87.1 us -> 77.7 us  [exchange_and_products(): pl.pallas_call(body, in_specs=[vmem] * 5 + [anywhere] * 3, out_specs=[vme...]
    pallas_call x1, Pallas kernels: 15.6 us -> 18.5 us  [weight_grads(): pl.pallas_call(body, grid=(pieces * per,), in_specs=[pl.BlockSpec((1, 1,...]
    unnamed x10 -> x12, local copies, waits for them, and re-layouts: 2.2 us -> 4.35 us
    pallas_call x1 -> x0, local copies, waits for them, and re-layouts: 1.86 us -> none  [exchange_and_products(): pl.pallas_call(body, in_specs=[vmem] * 5 + [anywhere] * 3, out_specs=[vme...]
where the time goes in v3:
time: 103 us; the launch traced here: 102 us
  Pallas kernels  96.2 us (93%)
  local copies, waits for them, and re-layouts  4.44 us (4%)
    pallas_call x1, Pallas kernels, exchange_and_products(): pl.pallas_call(body, in_specs=[vmem] * 5 + [anywhere] * 3, out_specs=[vme...  77.7 us
    pallas_call x1, Pallas kernels, weight_grads(): pl.pallas_call(body, grid=(pieces * per,), in_specs=[pl.BlockSpec((1, 1,...  18.5 us
    unnamed x12, local copies, waits for them, and re-layouts  4.35 us

profile of v3, /device:TPU:11, one launch (start us, length us, event | category | flops | bytes accessed | tf_op | source)
XLA Modules:
  0.0 102.1 jit_solution(7985500756160194959)
XLA Ops:
  0.6 0.0 copy-start
  0.7 0.7 copy-done
  1.4 0.1 fusion.1
  1.5 0.1 eq.39
  1.6 0.7 fusion.6.pick_ref
  2.3 0.7 copy.17.ids_ref
  3.0 1.4 %copy.16.w_ref = f32[128,2]{1,0:T(8,128)} copy(f32[128,2]{0,1:T(2,128)} %param.10) | data formatting | bytes 2048 | tf_op args[3]
  4.4 0.0 copy-start.1
  4.4 77.7 %shard_map.110 = (bf16[128,1536]{1,0:T(8,128)(2,1)}, bf16[128,1536]{1,0:T(8,128)(2,1)}, bf16[1024,128]{1,0:T(8,128)(2,1)}, bf16[128,1024]{1,0:T(8,128)(2,1)}, bf...) custom-call(bf16[32,128]{1,0:T(8,128)(2,1)} %fusion.6.pick_ref, s32[128,2]{1,0:T(8,128)} %copy.17.ids_ref, ...), custom_call_target="tpu_custom_call" | custom-call | flops 9663676416 | bytes 37748736 | tf_op jit(solution)/shard_map/pallas_call | solution.py:335
  82.1 0.0 copy-start.3
  82.1 0.0 copy-start.2
  82.1 18.5 %shard_map.111 = (bf16[6144,1024]{1,0:T(8,128)(2,1)}, bf16[6144,1024]{1,0:T(8,128)(2,1)}, bf16[1024,6144]{1,0:T(8,128)(2,1)}) custom-call(bf16[4,2,128,1536]{3,2,1,0:T(8,128)(2,1)} %get-tuple-element.16.tok_ref.grad_ref, bf16[4,2,128,1536]{3,2,1,0:T(8,128)(2,1)} %get-tuple-element.16.tok_ref.grad_ref, bf16[1024,128]{1,0:T(8,128)(2,1)} %get-tuple-element.17.hid_ref, ...), custom_call_target="tpu_custom_call" | custom-call | flops 4831838208 | bytes 37748736 | tf_op jit(solution)/shard_map/pallas_call | solution.py:36
  100.6 0.0 copy-done.3
  100.6 0.7 copy.20
  101.4 0.0 copy-done.2
  101.4 0.7 copy.21
  102.1 0.0 copy-done.1
  (3 shorter events, 0.0 us)
Async XLA Ops:
  0.6 0.7 copy-start
  4.4 97.7 %copy-start.1 = (s32[1024,2]{0,1:T(2,128)S(1)}, s32[1024,2]{0,1:T(2,128)}, u32[]{:S(2)}) copy-start(s32[1024,2]{0,1:T(2,128)} %param.9) | copy-start | bytes 24580
  82.1 18.5 %copy-start.3 = (bf16[128,1536]{1,0:T(8,128)(2,1)S(1)}, bf16[128,1536]{1,0:T(8,128)(2,1)}, u32[]{:S(2)}) copy-start(bf16[128,1536]{1,0:T(8,128)(2,1)} %get-tuple-element.28) | copy-start | bytes 1179652
  82.1 19.3 %copy-start.2 = (bf16[128,1536]{1,0:T(8,128)(2,1)S(1)}, bf16[128,1536]{1,0:T(8,128)(2,1)}, u32[]{:S(2)}) copy-start(bf16[128,1536]{1,0:T(8,128)(2,1)} %get-tuple-element.29) | copy-start | bytes 1179652

commit v4 on v3

--- a/solution.py
+++ b/solution.py
@@ -13,9 +13,8 @@
 def weight_grads(rows, hidden_t, dgate, dup):
     pieces, _, slots, width = rows.shape
     units = dgate.shape[1]
-    per = 4 if units % (64 * pieces) == 0 and width % 512 == 0 else 1
+    per = 2 if width % 256 == 0 else 1
     tile = width // per
-    high = units // (pieces * per)
 
     def body(tok_ref, grad_ref, hid_ref, dg_ref, du_ref, og_ref, ou_ref, od_ref):
         tok = tok_ref[0, 0]
@@ -26,19 +25,16 @@
         ou_ref[...] = lax.dot_general(
             tok, du_ref[...], contract, preferred_element_type=jnp.float32
         ).astype(jnp.bfloat16)
-        first = pl.program_id(0) * high
-        hid = hid_ref[pl.ds(pl.multiple_of(first, high), high), :]
-        for piece in range(pieces):
-            od_ref[:, piece * width : (piece + 1) * width] = jnp.dot(
-                hid, grad_ref[piece, 0], preferred_element_type=jnp.float32
-            ).astype(jnp.bfloat16)
+        od_ref[...] = jnp.dot(
+            hid_ref[...], grad_ref[0, 0], preferred_element_type=jnp.float32
+        ).astype(jnp.bfloat16)
 
     return pl.pallas_call(
         body,
         grid=(pieces * per,),
         in_specs=[
             pl.BlockSpec((1, 1, slots, tile), lambda i: (i // per, 0, 0, i % per)),
-            pl.BlockSpec((pieces, 1, slots, width), lambda i: (0, 1, 0, 0)),
+            pl.BlockSpec((1, 1, slots, tile), lambda i: (i // per, 1, 0, i % per)),
             pl.BlockSpec((units, slots), lambda i: (0, 0)),
             pl.BlockSpec((slots, units), lambda i: (0, 0)),
             pl.BlockSpec((slots, units), lambda i: (0, 0)),
@@ -46,7 +42,7 @@
         out_specs=[
             pl.BlockSpec((tile, units), lambda i: (i, 0)),
             pl.BlockSpec((tile, units), lambda i: (i, 0)),
-            pl.BlockSpec((high, pieces * width), lambda i: (i, 0)),
+            pl.BlockSpec((units, tile), lambda i: (0, i)),
         ],
         out_shape=[
             jax.ShapeDtypeStruct((pieces * width, units), jnp.bfloat16),

time: 103 us -> 99 us (0.961)
  Pallas kernels: 96.2 us -> 92.7 us
    pallas_call x1, Pallas kernels: 18.5 us -> 15 us  [weight_grads(): pl.pallas_call(body, grid=(pieces * per,), in_specs=[pl.BlockSpec((1, 1,...]
where the time goes in v4:
time: 99 us; the launch traced here: 98.6 us
  Pallas kernels  92.7 us (94%)
  local copies, waits for them, and re-layouts  4.44 us (4%)
    pallas_call x1, Pallas kernels, exchange_and_products(): pl.pallas_call(body, in_specs=[vmem] * 5 + [anywhere] * 3, out_specs=[vme...  77.7 us
    pallas_call x1, Pallas kernels, weight_grads(): pl.pallas_call(body, grid=(pieces * per,), in_specs=[pl.BlockSpec((1, 1,...  15 us
    unnamed x12, local copies, waits for them, and re-layouts  4.35 us

profile of v4, /device:TPU:11, one launch (start us, length us, event | category | flops | bytes accessed | tf_op | source)
XLA Modules:
  0.0 98.6 jit_solution(16366585093480149572)
XLA Ops:
  0.6 0.0 copy-start
  0.7 0.7 copy-done
  1.4 0.1 fusion.1
  1.5 0.1 eq.39
  1.6 0.7 fusion.6.pick_ref
  2.3 0.7 copy.17.ids_ref
  3.0 1.4 %copy.16.w_ref = f32[128,2]{1,0:T(8,128)} copy(f32[128,2]{0,1:T(2,128)} %param.10) | data formatting | bytes 2048 | tf_op args[3]
  4.4 0.0 copy-start.1
  4.4 77.7 %shard_map.110 = (bf16[128,1536]{1,0:T(8,128)(2,1)}, bf16[128,1536]{1,0:T(8,128)(2,1)}, bf16[1024,128]{1,0:T(8,128)(2,1)}, bf16[128,1024]{1,0:T(8,128)(2,1)}, bf...) custom-call(bf16[32,128]{1,0:T(8,128)(2,1)} %fusion.6.pick_ref, s32[128,2]{1,0:T(8,128)} %copy.17.ids_ref, ...), custom_call_target="tpu_custom_call" | custom-call | flops 9663676416 | bytes 37748736 | tf_op jit(solution)/shard_map/pallas_call | solution.py:331
  82.1 0.0 copy-start.3
  82.1 0.0 copy-start.2
  82.1 15.0 %shard_map.111 = (bf16[6144,1024]{1,0:T(8,128)(2,1)}, bf16[6144,1024]{1,0:T(8,128)(2,1)}, bf16[1024,6144]{1,0:T(8,128)(2,1)}) custom-call(bf16[4,2,128,1536]{3,2,1,0:T(8,128)(2,1)} %get-tuple-element.16.tok_ref.grad_ref, bf16[4,2,128,1536]{3,2,1,0:T(8,128)(2,1)} %get-tuple-element.16.tok_ref.grad_ref, bf16[1024,128]{1,0:T(8,128)(2,1)} %get-tuple-element.17.hid_ref, ...), custom_call_target="tpu_custom_call" | custom-call | flops 4831838208 | bytes 37748736 | tf_op jit(solution)/shard_map/pallas_call | solution.py:32
  97.1 0.0 copy-done.3
  97.1 0.7 copy.20
  97.9 0.0 copy-done.2
  97.9 0.7 copy.21
  98.6 0.0 copy-done.1
  (3 shorter events, 0.0 us)
Async XLA Ops:
  0.6 0.7 copy-start
  4.4 94.2 %copy-start.1 = (s32[1024,2]{0,1:T(2,128)S(1)}, s32[1024,2]{0,1:T(2,128)}, u32[]{:S(2)}) copy-start(s32[1024,2]{0,1:T(2,128)} %param.9) | copy-start | bytes 24580
  82.1 15.0 %copy-start.3 = (bf16[128,1536]{1,0:T(8,128)(2,1)S(1)}, bf16[128,1536]{1,0:T(8,128)(2,1)}, u32[]{:S(2)}) copy-start(bf16[128,1536]{1,0:T(8,128)(2,1)} %get-tuple-element.28) | copy-start | bytes 1179652
  82.1 15.8 %copy-start.2 = (bf16[128,1536]{1,0:T(8,128)(2,1)S(1)}, bf16[128,1536]{1,0:T(8,128)(2,1)}, u32[]{:S(2)}) copy-start(bf16[128,1536]{1,0:T(8,128)(2,1)} %get-tuple-element.29) | copy-start | bytes 1179652
